TPU v7x, 32 devices: a whole 2x2x4 slice. The times are simulated.
32 devices in a mesh: ctx: 8 (over z, core), heads: 4 (over y, x).
Axes of the slice: x: 2, y: 2, z: 4, core: 2. Of those that a mesh axis runs over, the one named last changes fastest.
Arguments:
- queries: bfloat16 [2048, 8192], P('ctx', 'heads'), may hold values from -6 to 6
- keys: bfloat16 [2048, 8192], P('ctx', 'heads'), may hold values from -6 to 6
- values: bfloat16 [2048, 8192], P('ctx', 'heads'), may hold values from -60 to 60
- hyena_inputs: bfloat16 [3, 2048, 8192], P(None, 'ctx', 'heads'), may hold values from -6 to 6
- hyena_filter: float32 [7, 8192], P(None, 'heads'), may hold values from -2.4 to 2.4
- norm_gain: float32 [8192], P('heads'), may hold values from 0.5 to 1.5
Outputs:
- mixed: bfloat16 [2048, 8192], P('ctx', 'heads')
All inputs are finite; a program needn't handle non-finite values.
Results may differ from a plain program's by a relative error of at most 0.009.
Values may be sent and summed in bfloat16 or wider, within the bound.
A program may use at most 64 MiB of HBM per device.

v0:
```python
import math

import jax
import jax.numpy as jnp
from jax import lax
from jax.sharding import PartitionSpec as P

DH = 128
WIDTH = 8192


def from_behind(array, axis, by):
    size = lax.axis_size(axis)
    pairs = [(i, i + by) for i in range(size) if 0 <= i + by < size]
    return lax.ppermute(array, axis, pairs)


def attend(half_state, query_block, query_place, key_block, value_block, key_place):
    numerator, maxima, totals = half_state
    score_scale = 1.0 / math.sqrt(query_block.shape[2])
    scores = (
        jnp.einsum("qhd,khd->qhk", query_block, key_block, preferred_element_type=jnp.float32)
        * score_scale
    )
    visible = key_place[None, None, :] <= query_place[:, None, None]
    scores = jnp.where(visible, scores, -1e30)
    row_top = jnp.maximum(maxima, jnp.max(scores, axis=2))
    rescale = jnp.exp(maxima - row_top)
    weights = jnp.where(visible, jnp.exp(scores - row_top[:, :, None]), 0.0)
    totals = totals * rescale + jnp.sum(weights, axis=2)
    summed = jnp.einsum(
        "qhk,khd->qhd",
        weights.astype(jnp.bfloat16),
        value_block,
        preferred_element_type=jnp.float32,
    )
    numerator = numerator * rescale[:, :, None] + summed
    return (numerator, row_top, totals)


def fresh_state(row_total, head_total, head_size):
    return (
        jnp.zeros((row_total, head_total, head_size), jnp.float32),
        jnp.full((row_total, head_total), -1e30, jnp.float32),
        jnp.zeros((row_total, head_total), jnp.float32),
    )


def cycle_attention(queries, keys, values):
    row_count, col_count = queries.shape
    head_count = col_count // DH
    half_rows = row_count // 2
    ctx_index = lax.axis_index("ctx")
    query_starts = (ctx_index * row_count, ctx_index * row_count + half_rows)
    query_heads = queries.reshape(row_count, head_count, DH)
    query_halves = (query_heads[:half_rows], query_heads[half_rows:])
    query_places = tuple(
        (query_starts[number] + jnp.arange(half_rows, dtype=jnp.int32) for number in range(2))
    )
    empty_state = fresh_state(half_rows, head_count, DH)
    key_rows = lax.all_gather(keys, "ctx", axis=0, tiled=True)
    value_rows = lax.all_gather(values, "ctx", axis=0, tiled=True)
    count = key_rows.shape[0]
    block_rows = math.gcd(count, half_rows)
    key_heads = key_rows.reshape(count, head_count, DH)
    value_heads = value_rows.reshape(count, head_count, DH)

    def inner(block_index, state):
        first = block_index * block_rows
        key_block = lax.dynamic_slice_in_dim(key_heads, first, block_rows, 0)
        value_block = lax.dynamic_slice_in_dim(value_heads, first, block_rows, 0)
        key_place = first + jnp.arange(block_rows, dtype=jnp.int32)
        updated = []
        for number in range(2):
            query_block = query_halves[number]
            query_place = query_places[number]

            def update(half_state):
                return attend(
                    half_state, query_block, query_place, key_block, value_block, key_place
                )

            needed = key_place[0] <= query_place[half_rows - 1]
            updated.append(lax.cond(needed, update, lambda half_state: half_state, state[number]))
        return tuple(updated)

    finished = lax.fori_loop(0, count // block_rows, inner, (empty_state, empty_state))
    halves_out = [finished[number][0] / finished[number][2][:, :, None] for number in range(2)]
    return jnp.concatenate(halves_out, axis=0).reshape(row_count, col_count).astype(jnp.bfloat16)


def on_device(queries, keys, values, hyena_inputs, hyena_filter, norm_gain):
    row_count, col_count = queries.shape
    rim_rows = hyena_filter.shape[0] - 1
    tail_rows = hyena_inputs[1:, row_count - rim_rows :, :]
    earlier = from_behind(tail_rows, "ctx", 1)
    joined = jnp.concatenate([earlier, hyena_inputs[1:]], axis=1)
    product = joined[0].astype(jnp.float32) * joined[1].astype(jnp.float32)
    convolved = jnp.zeros((row_count, col_count), jnp.float32)
    for filter_tap in range(rim_rows + 1):
        convolved = (
            convolved
            + hyena_filter[filter_tap][None, :]
            * product[rim_rows - filter_tap : rim_rows - filter_tap + row_count]
        )
    hyena_out = hyena_inputs[0].astype(jnp.float32) * convolved
    attention = cycle_attention(queries, keys, values)
    attention_wide = lax.optimization_barrier(attention).astype(jnp.float32)
    local_squares = jnp.sum(attention_wide * attention_wide, axis=1)
    square_total = lax.psum(local_squares, "heads")
    square_mean = square_total / WIDTH
    normed = attention_wide * lax.rsqrt(square_mean + 1e-06)[:, None] * norm_gain[None, :]
    return (normed + hyena_out).astype(jnp.bfloat16)


def solution(mesh):
    placed = (
        P("ctx", "heads"),
        P("ctx", "heads"),
        P("ctx", "heads"),
        P(None, "ctx", "heads"),
        P(None, "heads"),
        P("heads"),
    )
    return jax.shard_map(
        on_device, mesh=mesh, in_specs=placed, out_specs=P("ctx", "heads"), check_vma=False
    )
```

profile of v0, /device:TPU:25, one launch (start us, length us, event | category | flops | bytes accessed | tf_op | source)
XLA Modules:
  0.0 415.9 jit_solution(13052963984934846370)
XLA Ops:
  20.7 70.2 %all-gather.3.cloned.1.call-done = bf16[2048,2048]{0,1:T(8,128)(2,1)} async-done(((bf16[256,2048]{0,1:T(8,128)(2,1)}), bf16[2048,2048]{0,1:T(8,128)(2,1)}) %all-gather.3.cloned.1.call-update) | async-done | bytes 8388624 | tf_op jit(solution)/shard_map/all_gather | solution.py:61
  90.8 82.3 %all-gather.5.cloned.1.call-done = bf16[2048,2048]{0,1:T(8,128)(2,1)} async-done(((bf16[256,2048]{0,1:T(8,128)(2,1)}), bf16[2048,2048]{0,1:T(8,128)(2,1)}) %all-gather.5.cloned.1.call-update) | async-done | bytes 8388624 | tf_op jit(solution)/shard_map/all_gather | solution.py:62
  175.3 220.0 %while.23 = (s32[]{:T(128)}, f32[128,16,128]{2,0,1:T(8,128)}, f32[128,16]{0,1:T(8,128)S(1)}, f32[128,16]{0,1:T(8,128)S(1)}, f32[128,16,128]{2,0,1:T(8,128)}, /*i...) while((s32[]{:T(128)}, f32[128,16,128]{2,0,1:T(8,128)}, ...), condition=%wide.region_9.10_spmd, body=%wide.region_0.9_spmd.sunk | while | flops 274243712 | bytes 34999388 | solution.py:87
  180.5 3.7 conditional.5
  185.6 3.7 conditional.4
  194.5 3.7 conditional.5
  199.6 3.7 conditional.4
  208.5 3.7 conditional.5
  213.6 3.7 conditional.4
  222.5 3.7 conditional.5
  227.6 3.7 conditional.4
  236.4 3.7 conditional.5
  241.6 3.7 conditional.4
  250.4 3.7 conditional.5
  255.5 3.7 conditional.4
  264.4 3.7 conditional.5
  269.5 3.7 conditional.4
  278.4 3.7 conditional.5
  283.5 3.7 conditional.4
  292.4 3.7 conditional.5
  297.5 3.7 conditional.4
  306.3 3.7 conditional.5
  311.4 3.7 conditional.4
  320.3 3.7 conditional.5
  325.4 3.7 conditional.4
  334.3 3.7 conditional.5
  348.3 3.7 conditional.5
  362.2 3.7 conditional.5
  376.2 3.7 conditional.5
  390.2 3.7 conditional.5
  397.8 7.1 %psum.7 = f32[256]{0:T(256)S(1)} all-reduce(f32[256]{0:T(256)S(1)} %fusion.20), channel_id=1, replica_groups=mesh['ctx'=8,'heads'=4] {'heads'}, use_global_device_ids=true, to_apply=%region_11.12 | all-reduce | flops 256 | bytes 2048 | tf_op jit(solution)/shard_map/psum | solution.py:110
  405.0 4.1 fusion.23
  (481 shorter events, 227.0 us)
Async XLA Ops:
  6.5 2.4 copy-start.5
  6.5 84.3 %all-gather.3.cloned.1.call-start = ((), (), s32[]{:S(2)}) async-start(), calls=%async_computation | async-start | bytes 9437184 | tf_op jit(solution)/shard_map/all_gather | solution.py:61
  8.9 3.6 copy-start.7
  8.9 3.7 copy-start.6
  8.9 164.2 %all-gather.5.cloned.1.call-start = ((), (), s32[]{:S(2)}) async-start(), calls=%async_computation.1 | async-start | bytes 9437184 | tf_op jit(solution)/shard_map/all_gather | solution.py:62
  11.2 7.2 %collective-permute-start = (bf16[2,6,2048]{2,1,0:T(8,128)(2,1)S(1)}, bf16[2,6,2048]{2,1,0:T(8,128)(2,1)S(1)}, u32[]{:S(2)}, u32[]{:S(2)}) collective-permute-start(bf16[2,6,2048]{2,1,0:T(8,128)(2,1)S(1)} %slice.118), channel_id=1, source_target_pairs={{0,4},{4,8},{8,12},{12,16},{16,20},{20,24},{24,28},{1,5},{5,9},{9,... | collective-permute-start | bytes 147464 | tf_op jit(solution)/shard_map/ppermute | solution.py:15
  180.5 1.9 copy-start.2
  185.6 1.9 copy-start
  194.5 1.9 copy-start.2
  199.6 1.9 copy-start
  208.5 1.9 copy-start.2
  213.6 1.9 copy-start
  222.5 1.9 copy-start.2
  227.6 1.9 copy-start
  236.5 1.9 copy-start.2
  241.6 1.9 copy-start
  250.4 1.9 copy-start.2
  255.5 1.9 copy-start
  264.4 1.9 copy-start.2
  278.4 1.9 copy-start.2
  283.5 1.9 copy-start
  292.4 1.9 copy-start.2
  297.5 1.9 copy-start
  306.3 1.9 copy-start.2
  320.3 1.9 copy-start.2
  325.4 1.9 copy-start
  334.3 1.9 copy-start.2
  348.3 1.9 copy-start.2
  362.3 1.9 copy-start.2
  376.2 1.9 copy-start.2
  390.2 1.9 copy-start.2
  397.0 8.0 %copy-start.8 = (f32[2048]{0:T(1024)S(1)}, f32[2048]{0:T(1024)}, u32[]{:S(2)}) copy-start(f32[2048]{0:T(1024)} %param.17) | copy-start | bytes 24580
  (38 other events, 43.5 us)
Sparse Core Ops, SparseCore 0:
  9.0 81.7 all-gather.2
  92.4 80.6 all-gather.4
where the time goes:
time: 418 us; the launch traced here: 416 us
  waiting for transfers between devices  153 us (37%)
  local copies, waits for them, and re-layouts  124 us (30%)
  matrix products  73.2 us (18%)
  loops' own time  26.5 us (6%)
  other arithmetic  18 us (4%)
  between operations  13.6 us (3%)
  blocking collectives  7.14 us (2%)
    all_gather x1, waiting for transfers between devices, cycle_attention(): value_rows = lax.all_gather(values, 'ctx', axis=0, tiled=True)  82.3 us
    all_gather x1, waiting for transfers between devices, cycle_attention(): key_rows = lax.all_gather(keys, 'ctx', axis=0, tiled=True)  70.2 us
    dynamic_slice x32, local copies, waits for them, and re-layouts, inner(): value_block = lax.dynamic_slice_in_dim(value_heads, first, block_rows, 0)  55.2 us
    dot_general x31, matrix products, attend(): jnp.einsum('qhd,khd->qhk', query_block, key_block, preferred_element_type...  49.6 us
    cond x155, local copies, waits for them, and re-layouts  30.2 us
    another operation x1, loops' own time, cycle_attention(): lax.fori_loop(0, count // block_rows, inner, (empty_state, empty_state))  23.9 us
    dot_general x31, matrix products, attend(): jnp.einsum('qhk,khd->qhd', weights.astype(jnp.bfloat16), value_block, pre...  23.6 us
    slice x32, local copies, waits for them, and re-layouts, inner(): needed = key_place[0] <= query_place[half_rows - 1]  21.3 us
  transfers between devices with their start and end apart: 3, of which 2 were waited for; matrix products, arithmetic and copies ran while one was open for 2% of the time, Pallas kernels for 0%

commit v1 on v0

--- a/solution.py
+++ b/solution.py
@@ -1,12 +1,20 @@
+import functools
 import math
 
 import jax
 import jax.numpy as jnp
 from jax import lax
+from jax.experimental import pallas as pl
+from jax.experimental.pallas import tpu as pltpu
 from jax.sharding import PartitionSpec as P
 
 DH = 128
 WIDTH = 8192
+MESH = pl.DeviceIdType.MESH
+LOG2E = 1.4426950408889634
+CHUNK_HEADS = 2
+RIM = 16
+K_UP, V_UP, K_SIDE, V_SIDE, Q_NEAR, Q_FAR, O_NEAR, O_FAR, S_NEAR, S_FAR, SINGLES, SQUARES = range(12)
 
 
 def from_behind(array, axis, by):
@@ -89,7 +97,363 @@
     return jnp.concatenate(halves_out, axis=0).reshape(row_count, col_count).astype(jnp.bfloat16)
 
 
+def fused_kernel(
+    ctx_size, heads_size,
+    q_any, k_any, v_any, hy_any, filt, gain, out,
+    k_all, v_all, q_own, q_far, o_got, s_got, o_put, s_put, o_home, s_home,
+    att, hy, halo, prod, hyena, squares,
+    send_sem, recv_sem, local_sem,
+):
+    rows, cols = out.shape
+    chunks = cols // DH // CHUNK_HEADS
+    wide = CHUNK_HEADS * DH
+    ctx = lax.axis_index("ctx")
+    mine = lax.axis_index("heads")
+    core = lax.rem(ctx, 2)
+    place = ctx // 2
+    side = ctx + 1 - 2 * core
+    factor = LOG2E / math.sqrt(DH)
+
+    barrier = pltpu.get_barrier_semaphore()
+    for step in range(1, ctx_size):
+        pl.semaphore_signal(
+            barrier, inc=1, device_id={"ctx": lax.rem(ctx + step, ctx_size)}, device_id_type=MESH
+        )
+    for step in range(1, heads_size):
+        pl.semaphore_signal(
+            barrier, inc=1, device_id={"heads": lax.rem(mine + step, heads_size)}, device_id_type=MESH
+        )
+    pl.semaphore_wait(barrier, ctx_size + heads_size - 2)
+
+    def remote(src, dst, kind, at, target):
+        return pltpu.make_async_remote_copy(
+            src_ref=src, dst_ref=dst, send_sem=send_sem.at[kind, at], recv_sem=recv_sem.at[kind, at],
+            device_id={"ctx": target}, device_id_type=MESH,
+        )
+
+    def arrived(dst, kind, at):
+        remote(dst, dst, kind, at, side).wait_recv()
+
+    def sent(src, kind, at):
+        remote(src, src, kind, at, side).wait_send()
+
+    def lanes(chunk):
+        return pl.ds(pl.multiple_of(chunk * wide, wide), wide)
+
+    def head_lanes(head):
+        return pl.ds(pl.multiple_of(head * DH, DH), DH)
+
+    def each_chunk(body):
+        def step(chunk, carry):
+            body(chunk)
+            return carry
+
+        lax.fori_loop(0, chunks, step, 0)
+
+    tail = hy_any.at[pl.ds(1, 2), pl.ds(rows - RIM, RIM), :]
+
+    @pl.when(ctx < ctx_size - 1)
+    def _():
+        remote(tail, halo, SINGLES, 2, ctx + 1).start()
+
+    remote(k_any, k_all.at[2 + core], SINGLES, 0, side).start()
+    remote(v_any, v_all.at[2 + core], SINGLES, 1, side).start()
+
+    @pl.when(place == 0)
+    def _():
+        @each_chunk
+        def _(chunk):
+            at = lanes(chunk)
+            remote(k_any.at[:, at], k_all.at[core, :, at], K_UP, chunk, ctx + 2).start()
+            remote(v_any.at[:, at], v_all.at[core, :, at], V_UP, chunk, ctx + 2).start()
+
+    @pl.when(place == 2)
+    def _():
+        @each_chunk
+        def _(chunk):
+            at = lanes(chunk)
+            remote(q_any.at[:, at], q_far.at[0, :, at], Q_NEAR, chunk, ctx - 2).start()
+
+    @pl.when(place == 3)
+    def _():
+        @each_chunk
+        def _(chunk):
+            at = lanes(chunk)
+            remote(q_any.at[:, at], q_far.at[1, :, at], Q_FAR, chunk, ctx - 4).start()
+            remote(q_any.at[:, at], q_far.at[0, :, at], Q_NEAR, chunk, ctx - 2).start()
+
+    local = [
+        pltpu.make_async_copy(hy_any, hy, local_sem.at[0]),
+        pltpu.make_async_copy(k_any, k_all.at[2 + core], local_sem.at[1]),
+        pltpu.make_async_copy(v_any, v_all.at[2 + core], local_sem.at[2]),
+        pltpu.make_async_copy(q_any, q_own, local_sem.at[3]),
+    ]
+    for copy in local:
+        copy.start()
+
+    @pl.when(ctx == 0)
+    def _():
+        halo[...] = jnp.zeros_like(halo)
+
+    @pl.when(ctx > 0)
+    def _():
+        arrived(halo, SINGLES, 2)
+
+    local[0].wait()
+
+    @each_chunk
+    def _(chunk):
+        at = lanes(chunk)
+        prod[:RIM] = halo[0, :, at].astype(jnp.float32) * halo[1, :, at].astype(jnp.float32)
+        prod[RIM:] = hy[1, :, at].astype(jnp.float32) * hy[2, :, at].astype(jnp.float32)
+        taps = filt[:, at]
+        summed = taps[0:1] * prod[RIM : RIM + rows]
+        for tap in range(1, filt.shape[0]):
+            summed = summed + taps[tap : tap + 1] * prod[RIM - tap : RIM - tap + rows]
+        hyena[:, at] = hy[0, :, at].astype(jnp.float32) * summed
+
+    for copy in local[1:]:
+        copy.wait()
+    arrived(k_all.at[2], SINGLES, 0)
+    arrived(v_all.at[2], SINGLES, 1)
+    squares[mine] = jnp.zeros_like(squares[mine])
+
+    key_place = lax.broadcasted_iota(jnp.int32, (rows, rows), 0)
+    query_place = lax.broadcasted_iota(jnp.int32, (rows, rows), 1) + core * rows
+
+    def scores(slot, head, query):
+        return lax.dot_general(
+            k_all[slot, :, head_lanes(head)], query, (((1,), (1,)), ((), ())),
+            preferred_element_type=jnp.float32,
+        )
+
+    def turned(slot, head):
+        return v_all[slot, :, head_lanes(head)].T
+
+    def attend_some(head, query, slots, turned_values, masked):
+        tiles = [scores(slot, head, query) for slot in slots]
+        if masked:
+            tiles = [
+                jnp.where(key_place + (slot - 2) * rows <= query_place, tile, -1e30) if slot >= 2 else tile
+                for slot, tile in zip(slots, tiles)
+            ]
+        top = functools.reduce(jnp.maximum, [jnp.max(tile, axis=0, keepdims=True) for tile in tiles])
+        total, numerator = 0.0, 0.0
+        for tile, value in zip(tiles, turned_values):
+            weights = jnp.exp2((tile - top) * factor)
+            total = total + jnp.sum(weights, axis=0, keepdims=True)
+            numerator = numerator + jnp.dot(
+                value, weights.astype(jnp.bfloat16), preferred_element_type=jnp.float32
+            )
+        return numerator / total, top * factor + jnp.log(total) * LOG2E
+
+    def finish(head, value):
+        rounded = value.astype(jnp.bfloat16).astype(jnp.float32)
+        squares[mine] += jnp.sum((rounded * rounded).reshape(DH // 8, 8, rows), axis=0)
+        att[:, head_lanes(head)] = rounded.T.astype(jnp.bfloat16)
+
+    def head_rows(head):
+        return pl.ds(pl.multiple_of(head * DH, DH), DH)
+
+    def chunk_rows(chunk):
+        return pl.ds(pl.multiple_of(chunk * wide, wide), wide)
+
+    def partial_out(slot, chunk, index, head, result):
+        value, log_total = result
+        o_put[slot, head_rows(head), :] = value.astype(jnp.bfloat16)
+        s_put[slot, chunk, index : index + 1, :] = log_total
+
+    def send_out(slot, chunk, to_slot, target):
+        at = chunk_rows(chunk)
+        remote(o_put.at[slot, at], o_got.at[to_slot, at], O_NEAR + to_slot, chunk, target).start()
+        remote(s_put.at[slot, chunk], s_got.at[to_slot, chunk], S_NEAR + to_slot, chunk, target).start()
+
+    def own_query(head):
+        return q_own[:, head_lanes(head)]
+
+    @pl.when(place == 0)
+    def _():
+        @each_chunk
+        def _(chunk):
+            for index in range(CHUNK_HEADS):
+                head = chunk * CHUNK_HEADS + index
+                values = [turned(slot, head) for slot in (2, 3)]
+                finish(head, attend_some(head, own_query(head), (2, 3), values, True)[0])
+
+    @pl.when(place == 1)
+    def _():
+        s_put[...] = jnp.zeros_like(s_put)
+
+        @each_chunk
+        def _(chunk):
+            at = lanes(chunk)
+            arrived(k_all.at[core, :, at], K_UP, chunk)
+            remote(k_all.at[core, :, at], k_all.at[core, :, at], K_SIDE, chunk, side).start()
+            arrived(v_all.at[core, :, at], V_UP, chunk)
+            remote(v_all.at[core, :, at], v_all.at[core, :, at], V_SIDE, chunk, side).start()
+            arrived(q_far.at[0, :, at], Q_NEAR, chunk)
+            arrived(q_far.at[1, :, at], Q_FAR, chunk)
+            arrived(k_all.at[1 - core, :, at], K_SIDE, chunk)
+            arrived(v_all.at[1 - core, :, at], V_SIDE, chunk)
+            slots = (0, 1, 2, 3)
+            for index in range(CHUNK_HEADS):
+                head = chunk * CHUNK_HEADS + index
+                values = [turned(slot, head) for slot in slots]
+                for far in range(2):
+                    query = q_far[far, :, head_lanes(head)]
+                    partial_out(far, chunk, index, head, attend_some(head, query, slots, values, False))
+                finish(head, attend_some(head, own_query(head), slots, values, True)[0])
+            send_out(0, chunk, 0, ctx + 2)
+            send_out(1, chunk, 1, ctx + 4)
+
+    @pl.when(place == 2)
+    def _():
+        s_put[...] = jnp.zeros_like(s_put)
+
+        @each_chunk
+        def _(chunk):
+            arrived(q_far.at[0, :, lanes(chunk)], Q_NEAR, chunk)
+            for index in range(CHUNK_HEADS):
+                head = chunk * CHUNK_HEADS + index
+                values = [turned(slot, head) for slot in (2, 3)]
+                query = q_far[0, :, head_lanes(head)]
+                partial_out(0, chunk, index, head, attend_some(head, query, (2, 3), values, False))
+                value, log_total = attend_some(head, own_query(head), (2, 3), values, True)
+                o_home[head_rows(head), :] = value
+                s_home[chunk, index : index + 1, :] = log_total
+            send_out(0, chunk, 0, ctx + 2)
+
+    @pl.when(place == 3)
+    def _():
+        @each_chunk
+        def _(chunk):
+            for index in range(CHUNK_HEADS):
+                head = chunk * CHUNK_HEADS + index
+                values = [turned(slot, head) for slot in (2, 3)]
+                value, log_total = attend_some(head, own_query(head), (2, 3), values, True)
+                o_home[head_rows(head), :] = value
+                s_home[chunk, index : index + 1, :] = log_total
+
+    def merge(slots):
+        @each_chunk
+        def _(chunk):
+            for slot in slots:
+                arrived(o_got.at[slot, chunk_rows(chunk)], O_NEAR + slot, chunk)
+                arrived(s_got.at[slot, chunk], S_NEAR + slot, chunk)
+            for index in range(CHUNK_HEADS):
+                head = chunk * CHUNK_HEADS + index
+                logs = [s_home[chunk, index : index + 1, :]]
+                parts = [o_home[head_rows(head), :]]
+                for slot in slots:
+                    logs.append(s_got[slot, chunk, index : index + 1, :])
+                    parts.append(o_got[slot, head_rows(head), :].astype(jnp.float32))
+                top = functools.reduce(jnp.maximum, logs)
+                shares = [jnp.exp2(log - top) for log in logs]
+                inverse = 1.0 / sum(shares)
+                finish(head, sum(part * (share * inverse) for part, share in zip(parts, shares)))
+
+    pl.when(place == 2)(lambda: merge((0,)))
+    pl.when(place == 3)(lambda: merge((0, 1)))
+
+    def square_copy(step, slot):
+        return pltpu.make_async_remote_copy(
+            src_ref=squares.at[slot], dst_ref=squares.at[slot],
+            send_sem=send_sem.at[SQUARES, step], recv_sem=recv_sem.at[SQUARES, slot],
+            device_id={"heads": lax.rem(mine + step, heads_size)}, device_id_type=MESH,
+        )
+
+    for step in range(1, heads_size):
+        square_copy(step, mine).start()
+    for step in range(1, heads_size):
+        square_copy(step, lax.rem(mine + step, heads_size)).wait_recv()
+    square_total = squares[0]
+    for slot in range(1, heads_size):
+        square_total = square_total + squares[slot]
+    square_mean = jnp.sum(square_total, axis=0, keepdims=True) / (cols * heads_size)
+    scale = jnp.broadcast_to(lax.rsqrt(square_mean + 1e-06), (DH, rows)).T
+
+    def last(head, carry):
+        at = head_lanes(head)
+        out[:, at] = (att[:, at].astype(jnp.float32) * scale * gain[:, at] + hyena[:, at]).astype(jnp.bfloat16)
+        return carry
+
+    lax.fori_loop(0, cols // DH, last, 0)
+
+    for step in range(1, heads_size):
+        square_copy(step, mine).wait_send()
+
+    @pl.when(ctx < ctx_size - 1)
+    def _():
+        sent(tail, SINGLES, 2)
+
+    sent(k_any, SINGLES, 0)
+    sent(v_any, SINGLES, 1)
+
+    def sent_lanes(kinds):
+        @each_chunk
+        def _(chunk):
+            for kind in kinds:
+                sent(q_any.at[:, lanes(chunk)], kind, chunk)
+
+    def sent_out(slots):
+        @each_chunk
+        def _(chunk):
+            for slot in slots:
+                sent(o_put.at[slot, chunk_rows(chunk)], O_NEAR + slot, chunk)
+                sent(s_put.at[slot, chunk], S_NEAR + slot, chunk)
+
+    pl.when(place == 0)(lambda: sent_lanes((K_UP, V_UP)))
+    pl.when(place == 2)(lambda: sent_lanes((Q_NEAR,)))
+    pl.when(place == 3)(lambda: sent_lanes((Q_NEAR, Q_FAR)))
+    pl.when(place == 2)(lambda: sent_out((0,)))
+
+    @pl.when(place == 1)
+    def _():
+        sent_out((0, 1))
+        sent_lanes((K_SIDE, V_SIDE))
+
+
+def four_places(queries, keys, values, hyena_inputs, hyena_filter, norm_gain):
+    rows, cols = queries.shape
+    ctx_size, heads_size = lax.axis_size("ctx"), lax.axis_size("heads")
+    chunks = cols // DH // CHUNK_HEADS
+    bf16, f32 = jnp.bfloat16, jnp.float32
+    count = max(chunks, heads_size, 3)
+    return pl.pallas_call(
+        functools.partial(fused_kernel, ctx_size, heads_size),
+        out_shape=jax.ShapeDtypeStruct((rows, cols), bf16),
+        in_specs=[pl.BlockSpec(memory_space=pl.ANY)] * 4 + [pl.BlockSpec(memory_space=pltpu.VMEM)] * 2,
+        out_specs=pl.BlockSpec(memory_space=pltpu.VMEM),
+        scratch_shapes=[
+            pltpu.VMEM((4, rows, cols), bf16),
+            pltpu.VMEM((4, rows, cols), bf16),
+            pltpu.VMEM((rows, cols), bf16),
+            pltpu.VMEM((2, rows, cols), bf16),
+            pltpu.VMEM((2, cols, rows), bf16),
+            pltpu.VMEM((2, chunks, 8, rows), f32),
+            pltpu.VMEM((2, cols, rows), bf16),
+            pltpu.VMEM((2, chunks, 8, rows), f32),
+            pltpu.VMEM((cols, rows), f32),
+            pltpu.VMEM((chunks, 8, rows), f32),
+            pltpu.VMEM((rows, cols), bf16),
+            pltpu.VMEM(hyena_inputs.shape, bf16),
+            pltpu.VMEM((2, RIM, cols), bf16),
+            pltpu.VMEM((RIM + rows, CHUNK_HEADS * DH), f32),
+            pltpu.VMEM((rows, cols), f32),
+            pltpu.VMEM((heads_size, 8, rows), f32),
+            pltpu.SemaphoreType.DMA((12, count)),
+            pltpu.SemaphoreType.DMA((12, count)),
+            pltpu.SemaphoreType.DMA((4,)),
+        ],
+        compiler_params=pltpu.CompilerParams(
+            collective_id=0, has_side_effects=True, vmem_limit_bytes=50 * 1024 * 1024
+        ),
+    )(queries, keys, values, hyena_inputs, hyena_filter, norm_gain[None, :])
+
+
 def on_device(queries, keys, values, hyena_inputs, hyena_filter, norm_gain):
+    if lax.axis_size("ctx") == 2 * 4:
+        return four_places(queries, keys, values, hyena_inputs, hyena_filter, norm_gain)
     row_count, col_count = queries.shape
     rim_rows = hyena_filter.shape[0] - 1
     tail_rows = hyena_inputs[1:, row_count - rim_rows :, :]

time: 418 us -> 78.2 us (0.19)
  the two profiles are of different devices: /device:TPU:25 before, /device:TPU:24 now
where the time goes in v1:
time: 78.2 us; the launch traced here: 77.9 us
  Pallas kernels  72.9 us (93%)
  local copies, waits for them, and re-layouts  4.96 us (6%)
    pallas_call x1, Pallas kernels, four_places(): pl.pallas_call(functools.partial(fused_kernel, ctx_size, heads_size), out...  72.9 us
    unnamed x9, local copies, waits for them, and re-layouts  4.96 us

profile of v1, /device:TPU:24, one launch (start us, length us, event | category | flops | bytes accessed | tf_op | source)
XLA Modules:
  0.0 77.9 jit_solution(9734513597997736684)
XLA Ops:
  0.0 0.0 copy-start
  0.0 1.2 %copy-done = bf16[256,2048]{1,0:T(8,128)(2,1)S(1)} copy-done((bf16[256,2048]{1,0:T(8,128)(2,1)S(1)}, bf16[256,2048]{1,0:T(8,128)(2,1)}, u32[]{:S(2)}) %copy-start) | copy-done | bytes 1048600
  1.2 0.0 copy-start.1
  1.2 1.2 %copy-done.1 = bf16[256,2048]{1,0:T(8,128)(2,1)S(1)} copy-done((bf16[256,2048]{1,0:T(8,128)(2,1)S(1)}, bf16[256,2048]{1,0:T(8,128)(2,1)}, u32[]{:S(2)}) %copy-start.1) | copy-done | bytes 1048600
  2.5 0.0 copy-start.2
  2.5 0.8 %copy-done.2 = f32[7,2048]{1,0:T(8,128)S(1)} copy-done((f32[7,2048]{1,0:T(8,128)S(1)}, f32[7,2048]{1,0:T(8,128)}, u32[]{:S(2)}) %copy-start.2) | copy-done | bytes 57368
  3.3 0.0 copy-start.3
  3.3 0.7 copy-done.3
  4.0 72.9 %shard_map.64 = bf16[256,2048]{1,0:T(8,128)(2,1)S(1)} custom-call(bf16[256,2048]{1,0:T(8,128)(2,1)S(1)} %copy-done, bf16[256,2048]{1,0:T(8,128)(2,1)S(1)} %copy-done.1, bf16[256,2048]{1,0:T(8,128)(2,1)} %v_any.1, bf16[3,256,2048]{2,1,0:T(8,128)(2,1)} %hy_any.1, f32[7,2048]{1,0:T(8,128)S(1)} %copy-done.2, f32[1,2048]{1,0:T(1,128)S(1)} %bitcast.1), custom_call_target="tpu_custom_call" | custom-call | tf_op jit(solution)/shard_map/pallas_call | solution.py:422
  76.9 1.0 %copy.8 = bf16[256,2048]{1,0:T(8,128)(2,1)} copy(bf16[256,2048]{1,0:T(8,128)(2,1)S(1)} %shard_map.64) | data formatting | bytes 2097152
Async XLA Ops:
  0.0 1.2 %copy-start = (bf16[256,2048]{1,0:T(8,128)(2,1)S(1)}, bf16[256,2048]{1,0:T(8,128)(2,1)}, u32[]{:S(2)}) copy-start(bf16[256,2048]{1,0:T(8,128)(2,1)} %q_any.1) | copy-start | bytes 3145732
  1.2 1.2 %copy-start.1 = (bf16[256,2048]{1,0:T(8,128)(2,1)S(1)}, bf16[256,2048]{1,0:T(8,128)(2,1)}, u32[]{:S(2)}) copy-start(bf16[256,2048]{1,0:T(8,128)(2,1)} %k_any.1) | copy-start | bytes 3145732
  2.5 0.8 %copy-start.2 = (f32[7,2048]{1,0:T(8,128)S(1)}, f32[7,2048]{1,0:T(8,128)}, u32[]{:S(2)}) copy-start(f32[7,2048]{1,0:T(8,128)} %filt.1) | copy-start | bytes 172036
  3.3 0.7 copy-start.3

commit v2 on v1

--- a/solution.py
+++ b/solution.py
@@ -13,6 +13,7 @@
 MESH = pl.DeviceIdType.MESH
 LOG2E = 1.4426950408889634
 CHUNK_HEADS = 2
+DEPTH = 2
 RIM = 16
 K_UP, V_UP, K_SIDE, V_SIDE, Q_NEAR, Q_FAR, O_NEAR, O_FAR, S_NEAR, S_FAR, SINGLES, SQUARES = range(12)
 
@@ -99,9 +100,9 @@
 
 def fused_kernel(
     ctx_size, heads_size,
-    q_any, k_any, v_any, hy_any, filt, gain, out,
+    q_any, k_any, v_any, hy_any, filt_any, gain_any, out,
     k_all, v_all, q_own, q_far, o_got, s_got, o_put, s_put, o_home, s_home,
-    att, hy, halo, prod, hyena, squares,
+    att, hy, halo, prod, hyena, squares, filt, gain,
     send_sem, recv_sem, local_sem,
 ):
     rows, cols = out.shape
@@ -114,6 +115,14 @@
     side = ctx + 1 - 2 * core
     factor = LOG2E / math.sqrt(DH)
 
+    local = [
+        pltpu.make_async_copy(hy_any, hy, local_sem.at[0]),
+        pltpu.make_async_copy(filt_any, filt, local_sem.at[1]),
+        pltpu.make_async_copy(k_any, k_all.at[2 + core], local_sem.at[2]),
+        pltpu.make_async_copy(v_any, v_all.at[2 + core], local_sem.at[3]),
+        pltpu.make_async_copy(q_any, q_own, local_sem.at[4]),
+        pltpu.make_async_copy(gain_any, gain, local_sem.at[5]),
+    ]
     barrier = pltpu.get_barrier_semaphore()
     for step in range(1, ctx_size):
         pl.semaphore_signal(
@@ -123,6 +132,8 @@
         pl.semaphore_signal(
             barrier, inc=1, device_id={"heads": lax.rem(mine + step, heads_size)}, device_id_type=MESH
         )
+    for copy in local:
+        copy.start()
     pl.semaphore_wait(barrier, ctx_size + heads_size - 2)
 
     def remote(src, dst, kind, at, target):
@@ -159,37 +170,38 @@
     remote(k_any, k_all.at[2 + core], SINGLES, 0, side).start()
     remote(v_any, v_all.at[2 + core], SINGLES, 1, side).start()
 
-    @pl.when(place == 0)
-    def _():
-        @each_chunk
-        def _(chunk):
-            at = lanes(chunk)
-            remote(k_any.at[:, at], k_all.at[core, :, at], K_UP, chunk, ctx + 2).start()
-            remote(v_any.at[:, at], v_all.at[core, :, at], V_UP, chunk, ctx + 2).start()
-
-    @pl.when(place == 2)
-    def _():
-        @each_chunk
-        def _(chunk):
-            at = lanes(chunk)
-            remote(q_any.at[:, at], q_far.at[0, :, at], Q_NEAR, chunk, ctx - 2).start()
-
-    @pl.when(place == 3)
-    def _():
-        @each_chunk
-        def _(chunk):
-            at = lanes(chunk)
-            remote(q_any.at[:, at], q_far.at[1, :, at], Q_FAR, chunk, ctx - 4).start()
-            remote(q_any.at[:, at], q_far.at[0, :, at], Q_NEAR, chunk, ctx - 2).start()
-
-    local = [
-        pltpu.make_async_copy(hy_any, hy, local_sem.at[0]),
-        pltpu.make_async_copy(k_any, k_all.at[2 + core], local_sem.at[1]),
-        pltpu.make_async_copy(v_any, v_all.at[2 + core], local_sem.at[2]),
-        pltpu.make_async_copy(q_any, q_own, local_sem.at[3]),
-    ]
-    for copy in local:
-        copy.start()
+    def up_copies(chunk):
+        at = lanes(chunk)
+        return (
+            remote(k_any.at[:, at], k_all.at[core, :, at], K_UP, chunk, ctx + 2),
+            remote(v_any.at[:, at], v_all.at[core, :, at], V_UP, chunk, ctx + 2),
+        )
+
+    def near_copies(chunk):
+        at = lanes(chunk)
+        return (remote(q_any.at[:, at], q_far.at[0, :, at], Q_NEAR, chunk, ctx - 2),)
+
+    def far_copies(chunk):
+        at = lanes(chunk)
+        return (remote(q_any.at[:, at], q_far.at[1, :, at], Q_FAR, chunk, ctx - 4),) + near_copies(chunk)
+
+    def begin(copies, depth):
+        for chunk in range(depth):
+            for copy in copies(chunk):
+                copy.start()
+
+    def follow(copies, depth, chunk):
+        for copy in copies(chunk):
+            copy.wait_send()
+
+        @pl.when(chunk + depth < chunks)
+        def _():
+            for copy in copies(chunk + depth):
+                copy.start()
+
+    pl.when(place == 0)(lambda: begin(up_copies, DEPTH))
+    pl.when(place == 2)(lambda: begin(near_copies, 2 * DEPTH))
+    pl.when(place == 3)(lambda: begin(far_copies, DEPTH))
 
     @pl.when(ctx == 0)
     def _():
@@ -199,7 +211,8 @@
     def _():
         arrived(halo, SINGLES, 2)
 
-    local[0].wait()
+    for copy in local[:2]:
+        copy.wait()
 
     @each_chunk
     def _(chunk):
@@ -212,7 +225,7 @@
             summed = summed + taps[tap : tap + 1] * prod[RIM - tap : RIM - tap + rows]
         hyena[:, at] = hy[0, :, at].astype(jnp.float32) * summed
 
-    for copy in local[1:]:
+    for copy in local[2:]:
         copy.wait()
     arrived(k_all.at[2], SINGLES, 0)
     arrived(v_all.at[2], SINGLES, 1)
@@ -275,6 +288,7 @@
     def _():
         @each_chunk
         def _(chunk):
+            follow(up_copies, DEPTH, chunk)
             for index in range(CHUNK_HEADS):
                 head = chunk * CHUNK_HEADS + index
                 values = [turned(slot, head) for slot in (2, 3)]
@@ -296,15 +310,16 @@
             arrived(k_all.at[1 - core, :, at], K_SIDE, chunk)
             arrived(v_all.at[1 - core, :, at], V_SIDE, chunk)
             slots = (0, 1, 2, 3)
-            for index in range(CHUNK_HEADS):
-                head = chunk * CHUNK_HEADS + index
-                values = [turned(slot, head) for slot in slots]
-                for far in range(2):
+            heads = [chunk * CHUNK_HEADS + index for index in range(CHUNK_HEADS)]
+            values = [[turned(slot, head) for slot in slots] for head in heads]
+            for far in (1, 0):
+                for index, head in enumerate(heads):
                     query = q_far[far, :, head_lanes(head)]
-                    partial_out(far, chunk, index, head, attend_some(head, query, slots, values, False))
-                finish(head, attend_some(head, own_query(head), slots, values, True)[0])
-            send_out(0, chunk, 0, ctx + 2)
-            send_out(1, chunk, 1, ctx + 4)
+                    result = attend_some(head, query, slots, values[index], False)
+                    partial_out(far, chunk, index, head, result)
+                send_out(far, chunk, far, ctx + 2 + 2 * far)
+            for index, head in enumerate(heads):
+                finish(head, attend_some(head, own_query(head), slots, values[index], True)[0])
 
     @pl.when(place == 2)
     def _():
@@ -312,6 +327,7 @@
 
         @each_chunk
         def _(chunk):
+            follow(near_copies, 2 * DEPTH, chunk)
             arrived(q_far.at[0, :, lanes(chunk)], Q_NEAR, chunk)
             for index in range(CHUNK_HEADS):
                 head = chunk * CHUNK_HEADS + index
@@ -327,6 +343,7 @@
     def _():
         @each_chunk
         def _(chunk):
+            follow(far_copies, DEPTH, chunk)
             for index in range(CHUNK_HEADS):
                 head = chunk * CHUNK_HEADS + index
                 values = [turned(slot, head) for slot in (2, 3)]
@@ -402,9 +419,6 @@
                 sent(o_put.at[slot, chunk_rows(chunk)], O_NEAR + slot, chunk)
                 sent(s_put.at[slot, chunk], S_NEAR + slot, chunk)
 
-    pl.when(place == 0)(lambda: sent_lanes((K_UP, V_UP)))
-    pl.when(place == 2)(lambda: sent_lanes((Q_NEAR,)))
-    pl.when(place == 3)(lambda: sent_lanes((Q_NEAR, Q_FAR)))
     pl.when(place == 2)(lambda: sent_out((0,)))
 
     @pl.when(place == 1)
@@ -422,7 +436,7 @@
     return pl.pallas_call(
         functools.partial(fused_kernel, ctx_size, heads_size),
         out_shape=jax.ShapeDtypeStruct((rows, cols), bf16),
-        in_specs=[pl.BlockSpec(memory_space=pl.ANY)] * 4 + [pl.BlockSpec(memory_space=pltpu.VMEM)] * 2,
+        in_specs=[pl.BlockSpec(memory_space=pltpu.HBM)] * 6,
         out_specs=pl.BlockSpec(memory_space=pltpu.VMEM),
         scratch_shapes=[
             pltpu.VMEM((4, rows, cols), bf16),
@@ -441,12 +455,14 @@
             pltpu.VMEM((RIM + rows, CHUNK_HEADS * DH), f32),
             pltpu.VMEM((rows, cols), f32),
             pltpu.VMEM((heads_size, 8, rows), f32),
+            pltpu.VMEM(hyena_filter.shape, f32),
+            pltpu.VMEM((1, cols), f32),
             pltpu.SemaphoreType.DMA((12, count)),
             pltpu.SemaphoreType.DMA((12, count)),
-            pltpu.SemaphoreType.DMA((4,)),
+            pltpu.SemaphoreType.DMA((6,)),
         ],
         compiler_params=pltpu.CompilerParams(
-            collective_id=0, has_side_effects=True, vmem_limit_bytes=50 * 1024 * 1024
+            collective_id=0, has_side_effects=True, vmem_limit_bytes=63 * 1024 * 1024
         ),
     )(queries, keys, values, hyena_inputs, hyena_filter, norm_gain[None, :])
 

time: 78.2 us -> 74.7 us (0.955)
  the two profiles are of different devices: /device:TPU:24 before, /device:TPU:16 now
where the time goes in v2:
time: 74.7 us; the launch traced here: 74.6 us
  Pallas kernels  72.3 us (97%)
  local copies, waits for them, and re-layouts  2.3 us (3%)
    pallas_call x1, Pallas kernels, four_places(): pl.pallas_call(functools.partial(fused_kernel, ctx_size, heads_size), out...  72.3 us
    unnamed x1, local copies, waits for them, and re-layouts  2.3 us

profile of v2, /device:TPU:16, one launch (start us, length us, event | category | flops | bytes accessed | tf_op | source)
XLA Modules:
  0.0 74.6 jit_solution(16253902546388541380)
XLA Ops:
  0.0 72.3 %shard_map.64 = bf16[256,2048]{1,0:T(8,128)(2,1)} custom-call(bf16[256,2048]{1,0:T(8,128)(2,1)} %q_any.1, bf16[256,2048]{1,0:T(8,128)(2,1)} %k_any.1, bf16[256,2048]{1,0:T(8,128)(2,1)} %v_any.1, bf16[3,256,2048]{2,1,0:T(8,128)(2,1)} %hy_any.1, f32[7,2048]{1,0:T(8,128)} %filt_any.1, f32[1,2048]{1,0:T(1,128)} %bitcast.1), custom_call_target="tpu_custom_call" | custom-call | tf_op jit(solution)/shard_map/pallas_call | solution.py:436
  72.3 2.3 %copy.8 = bf16[256,2048]{1,0:T(8,128)(2,1)} copy(bf16[256,2048]{1,0:T(8,128)(2,1)} %shard_map.64) | data formatting | bytes 2097152

commit v3 on v2

--- a/solution.py
+++ b/solution.py
@@ -13,7 +13,7 @@
 MESH = pl.DeviceIdType.MESH
 LOG2E = 1.4426950408889634
 CHUNK_HEADS = 2
-DEPTH = 2
+DEPTH = 4
 RIM = 16
 K_UP, V_UP, K_SIDE, V_SIDE, Q_NEAR, Q_FAR, O_NEAR, O_FAR, S_NEAR, S_FAR, SINGLES, SQUARES = range(12)
 
@@ -243,14 +243,16 @@
     def turned(slot, head):
         return v_all[slot, :, head_lanes(head)].T
 
-    def attend_some(head, query, slots, turned_values, masked):
+    def masked_scores(head, query, slots, masked):
         tiles = [scores(slot, head, query) for slot in slots]
         if masked:
             tiles = [
                 jnp.where(key_place + (slot - 2) * rows <= query_place, tile, -1e30) if slot >= 2 else tile
                 for slot, tile in zip(slots, tiles)
             ]
-        top = functools.reduce(jnp.maximum, [jnp.max(tile, axis=0, keepdims=True) for tile in tiles])
+        return tiles, functools.reduce(jnp.maximum, [jnp.max(tile, axis=0, keepdims=True) for tile in tiles])
+
+    def weigh(tiles, top, turned_values):
         total, numerator = 0.0, 0.0
         for tile, value in zip(tiles, turned_values):
             weights = jnp.exp2((tile - top) * factor)
@@ -259,6 +261,9 @@
                 value, weights.astype(jnp.bfloat16), preferred_element_type=jnp.float32
             )
         return numerator / total, top * factor + jnp.log(total) * LOG2E
+
+    def attend_some(head, query, slots, turned_values, masked):
+        return weigh(*masked_scores(head, query, slots, masked), turned_values)
 
     def finish(head, value):
         rounded = value.astype(jnp.bfloat16).astype(jnp.float32)
@@ -312,14 +317,25 @@
             slots = (0, 1, 2, 3)
             heads = [chunk * CHUNK_HEADS + index for index in range(CHUNK_HEADS)]
             values = [[turned(slot, head) for slot in slots] for head in heads]
-            for far in (1, 0):
-                for index, head in enumerate(heads):
-                    query = q_far[far, :, head_lanes(head)]
-                    result = attend_some(head, query, slots, values[index], False)
-                    partial_out(far, chunk, index, head, result)
-                send_out(far, chunk, far, ctx + 2 + 2 * far)
-            for index, head in enumerate(heads):
-                finish(head, attend_some(head, own_query(head), slots, values[index], True)[0])
+            works = [(far, index) for far in (1, 0, None) for index in range(CHUNK_HEADS)]
+
+            def begin_work(far, index):
+                head = heads[index]
+                query = own_query(head) if far is None else q_far[far, :, head_lanes(head)]
+                return masked_scores(head, query, slots, far is None)
+
+            ready = begin_work(*works[0])
+            for number, (far, index) in enumerate(works):
+                current = ready
+                if number + 1 < len(works):
+                    ready = begin_work(*works[number + 1])
+                result = weigh(*current, values[index])
+                if far is None:
+                    finish(heads[index], result[0])
+                    continue
+                partial_out(far, chunk, index, heads[index], result)
+                if index == CHUNK_HEADS - 1:
+                    send_out(far, chunk, far, ctx + 2 + 2 * far)
 
     @pl.when(place == 2)
     def _():

time: 74.7 us -> 74.1 us (level)
  no operation moved by 1% of the time
where the time goes in v3:
time: 74.1 us; the launch traced here: 74 us
  Pallas kernels  71.7 us (97%)
  local copies, waits for them, and re-layouts  2.3 us (3%)
    pallas_call x1, Pallas kernels, four_places(): pl.pallas_call(functools.partial(fused_kernel, ctx_size, heads_size), out...  71.7 us
    unnamed x1, local copies, waits for them, and re-layouts  2.3 us

profile of v3, /device:TPU:16, one launch (start us, length us, event | category | flops | bytes accessed | tf_op | source)
XLA Modules:
  0.0 74.0 jit_solution(1251346683698862780)
XLA Ops:
  0.0 71.7 %shard_map.64 = bf16[256,2048]{1,0:T(8,128)(2,1)} custom-call(bf16[256,2048]{1,0:T(8,128)(2,1)} %q_any.1, bf16[256,2048]{1,0:T(8,128)(2,1)} %k_any.1, bf16[256,2048]{1,0:T(8,128)(2,1)} %v_any.1, bf16[3,256,2048]{2,1,0:T(8,128)(2,1)} %hy_any.1, f32[7,2048]{1,0:T(8,128)} %filt_any.1, f32[1,2048]{1,0:T(1,128)} %bitcast.1), custom_call_target="tpu_custom_call" | custom-call | tf_op jit(solution)/shard_map/pallas_call | solution.py:452
  71.7 2.3 %copy.8 = bf16[256,2048]{1,0:T(8,128)(2,1)} copy(bf16[256,2048]{1,0:T(8,128)(2,1)} %shard_map.64) | data formatting | bytes 2097152

commit v4 on v3

--- a/solution.py
+++ b/solution.py
@@ -12,8 +12,9 @@
 WIDTH = 8192
 MESH = pl.DeviceIdType.MESH
 LOG2E = 1.4426950408889634
-CHUNK_HEADS = 2
+CHUNK_HEADS = 1
 DEPTH = 4
+LAG = 6
 RIM = 16
 K_UP, V_UP, K_SIDE, V_SIDE, Q_NEAR, Q_FAR, O_NEAR, O_FAR, S_NEAR, S_FAR, SINGLES, SQUARES = range(12)
 
@@ -123,6 +124,8 @@
         pltpu.make_async_copy(q_any, q_own, local_sem.at[4]),
         pltpu.make_async_copy(gain_any, gain, local_sem.at[5]),
     ]
+    for copy in local[2:5] + local[:2] + local[5:]:
+        copy.start()
     barrier = pltpu.get_barrier_semaphore()
     for step in range(1, ctx_size):
         pl.semaphore_signal(
@@ -132,9 +135,9 @@
         pl.semaphore_signal(
             barrier, inc=1, device_id={"heads": lax.rem(mine + step, heads_size)}, device_id_type=MESH
         )
-    for copy in local:
-        copy.start()
     pl.semaphore_wait(barrier, ctx_size + heads_size - 2)
+    for copy in local[2:5]:
+        copy.wait()
 
     def remote(src, dst, kind, at, target):
         return pltpu.make_async_remote_copy(
@@ -163,27 +166,27 @@
 
     tail = hy_any.at[pl.ds(1, 2), pl.ds(rows - RIM, RIM), :]
 
-    @pl.when(ctx < ctx_size - 1)
-    def _():
+    def send_tail():
         remote(tail, halo, SINGLES, 2, ctx + 1).start()
 
+    pl.when((ctx < ctx_size - 1) & (ctx != 1))(send_tail)
     remote(k_any, k_all.at[2 + core], SINGLES, 0, side).start()
     remote(v_any, v_all.at[2 + core], SINGLES, 1, side).start()
 
     def up_copies(chunk):
         at = lanes(chunk)
         return (
-            remote(k_any.at[:, at], k_all.at[core, :, at], K_UP, chunk, ctx + 2),
-            remote(v_any.at[:, at], v_all.at[core, :, at], V_UP, chunk, ctx + 2),
+            remote(k_all.at[2 + core, :, at], k_all.at[core, :, at], K_UP, chunk, ctx + 2),
+            remote(v_all.at[2 + core, :, at], v_all.at[core, :, at], V_UP, chunk, ctx + 2),
         )
 
     def near_copies(chunk):
         at = lanes(chunk)
-        return (remote(q_any.at[:, at], q_far.at[0, :, at], Q_NEAR, chunk, ctx - 2),)
+        return (remote(q_own.at[:, at], q_far.at[0, :, at], Q_NEAR, chunk, ctx - 2),)
 
     def far_copies(chunk):
         at = lanes(chunk)
-        return (remote(q_any.at[:, at], q_far.at[1, :, at], Q_FAR, chunk, ctx - 4),) + near_copies(chunk)
+        return (remote(q_own.at[:, at], q_far.at[1, :, at], Q_FAR, chunk, ctx - 4),) + near_copies(chunk)
 
     def begin(copies, depth):
         for chunk in range(depth):
@@ -201,32 +204,34 @@
 
     pl.when(place == 0)(lambda: begin(up_copies, DEPTH))
     pl.when(place == 2)(lambda: begin(near_copies, 2 * DEPTH))
-    pl.when(place == 3)(lambda: begin(far_copies, DEPTH))
-
-    @pl.when(ctx == 0)
-    def _():
-        halo[...] = jnp.zeros_like(halo)
-
-    @pl.when(ctx > 0)
-    def _():
-        arrived(halo, SINGLES, 2)
-
-    for copy in local[:2]:
-        copy.wait()
-
-    @each_chunk
-    def _(chunk):
-        at = lanes(chunk)
-        prod[:RIM] = halo[0, :, at].astype(jnp.float32) * halo[1, :, at].astype(jnp.float32)
-        prod[RIM:] = hy[1, :, at].astype(jnp.float32) * hy[2, :, at].astype(jnp.float32)
-        taps = filt[:, at]
-        summed = taps[0:1] * prod[RIM : RIM + rows]
-        for tap in range(1, filt.shape[0]):
-            summed = summed + taps[tap : tap + 1] * prod[RIM - tap : RIM - tap + rows]
-        hyena[:, at] = hy[0, :, at].astype(jnp.float32) * summed
-
-    for copy in local[2:]:
-        copy.wait()
+    pl.when(place == 3)(lambda: begin(far_copies, 2 * DEPTH))
+
+    def gate():
+        @pl.when(ctx == 0)
+        def _():
+            halo[...] = jnp.zeros_like(halo)
+
+        @pl.when(ctx > 0)
+        def _():
+            arrived(halo, SINGLES, 2)
+
+        for copy in local[:2]:
+            copy.wait()
+
+        @each_chunk
+        def _(chunk):
+            at = lanes(chunk)
+            prod[:RIM] = halo[0, :, at].astype(jnp.float32) * halo[1, :, at].astype(jnp.float32)
+            prod[RIM:] = hy[1, :, at].astype(jnp.float32) * hy[2, :, at].astype(jnp.float32)
+            taps = filt[:, at]
+            summed = taps[0:1] * prod[RIM : RIM + rows]
+            for tap in range(1, filt.shape[0]):
+                summed = summed + taps[tap : tap + 1] * prod[RIM - tap : RIM - tap + rows]
+            hyena[:, at] = hy[0, :, at].astype(jnp.float32) * summed
+
+    pl.when(place != 1)(gate)
+
+    local[5].wait()
     arrived(k_all.at[2], SINGLES, 0)
     arrived(v_all.at[2], SINGLES, 1)
     squares[mine] = jnp.zeros_like(squares[mine])
@@ -286,6 +291,32 @@
         remote(o_put.at[slot, at], o_got.at[to_slot, at], O_NEAR + to_slot, chunk, target).start()
         remote(s_put.at[slot, chunk], s_got.at[to_slot, chunk], S_NEAR + to_slot, chunk, target).start()
 
+    def merge(slots, chunk):
+        for slot in slots:
+            arrived(o_got.at[slot, chunk_rows(chunk)], O_NEAR + slot, chunk)
+            arrived(s_got.at[slot, chunk], S_NEAR + slot, chunk)
+        for index in range(CHUNK_HEADS):
+            head = chunk * CHUNK_HEADS + index
+            logs = [s_home[chunk, index : index + 1, :]]
+            parts = [o_home[head_rows(head), :]]
+            for slot in slots:
+                logs.append(s_got[slot, chunk, index : index + 1, :])
+                parts.append(o_got[slot, head_rows(head), :].astype(jnp.float32))
+            top = functools.reduce(jnp.maximum, logs)
+            shares = [jnp.exp2(log - top) for log in logs]
+            inverse = 1.0 / sum(shares)
+            finish(head, sum(part * (share * inverse) for part, share in zip(parts, shares)))
+
+    def merge_behind(slots, chunk):
+        pl.when(chunk >= LAG)(lambda: merge(slots, chunk - LAG))
+
+    def merge_rest(slots):
+        def step(chunk, carry):
+            merge(slots, chunk)
+            return carry
+
+        lax.fori_loop(max(chunks - LAG, 0), chunks, step, 0)
+
     def own_query(head):
         return q_own[:, head_lanes(head)]
 
@@ -299,10 +330,10 @@
                 values = [turned(slot, head) for slot in (2, 3)]
                 finish(head, attend_some(head, own_query(head), (2, 3), values, True)[0])
 
+        pl.when(core == 1)(send_tail)
+
     @pl.when(place == 1)
     def _():
-        s_put[...] = jnp.zeros_like(s_put)
-
         @each_chunk
         def _(chunk):
             at = lanes(chunk)
@@ -337,10 +368,10 @@
                 if index == CHUNK_HEADS - 1:
                     send_out(far, chunk, far, ctx + 2 + 2 * far)
 
+        gate()
+
     @pl.when(place == 2)
     def _():
-        s_put[...] = jnp.zeros_like(s_put)
-
         @each_chunk
         def _(chunk):
             follow(near_copies, 2 * DEPTH, chunk)
@@ -354,39 +385,24 @@
                 o_home[head_rows(head), :] = value
                 s_home[chunk, index : index + 1, :] = log_total
             send_out(0, chunk, 0, ctx + 2)
+            merge_behind((0,), chunk)
+
+        merge_rest((0,))
 
     @pl.when(place == 3)
     def _():
         @each_chunk
         def _(chunk):
-            follow(far_copies, DEPTH, chunk)
+            follow(far_copies, 2 * DEPTH, chunk)
             for index in range(CHUNK_HEADS):
                 head = chunk * CHUNK_HEADS + index
                 values = [turned(slot, head) for slot in (2, 3)]
                 value, log_total = attend_some(head, own_query(head), (2, 3), values, True)
                 o_home[head_rows(head), :] = value
                 s_home[chunk, index : index + 1, :] = log_total
-
-    def merge(slots):
-        @each_chunk
-        def _(chunk):
-            for slot in slots:
-                arrived(o_got.at[slot, chunk_rows(chunk)], O_NEAR + slot, chunk)
-                arrived(s_got.at[slot, chunk], S_NEAR + slot, chunk)
-            for index in range(CHUNK_HEADS):
-                head = chunk * CHUNK_HEADS + index
-                logs = [s_home[chunk, index : index + 1, :]]
-                parts = [o_home[head_rows(head), :]]
-                for slot in slots:
-                    logs.append(s_got[slot, chunk, index : index + 1, :])
-                    parts.append(o_got[slot, head_rows(head), :].astype(jnp.float32))
-                top = functools.reduce(jnp.maximum, logs)
-                shares = [jnp.exp2(log - top) for log in logs]
-                inverse = 1.0 / sum(shares)
-                finish(head, sum(part * (share * inverse) for part, share in zip(parts, shares)))
-
-    pl.when(place == 2)(lambda: merge((0,)))
-    pl.when(place == 3)(lambda: merge((0, 1)))
+            merge_behind((0, 1), chunk)
+
+        merge_rest((0, 1))
 
     def square_copy(step, slot):
         return pltpu.make_async_remote_copy(
@@ -460,11 +476,11 @@
             pltpu.VMEM((rows, cols), bf16),
             pltpu.VMEM((2, rows, cols), bf16),
             pltpu.VMEM((2, cols, rows), bf16),
-            pltpu.VMEM((2, chunks, 8, rows), f32),
+            pltpu.VMEM((2, chunks, CHUNK_HEADS, rows), f32),
             pltpu.VMEM((2, cols, rows), bf16),
-            pltpu.VMEM((2, chunks, 8, rows), f32),
+            pltpu.VMEM((2, chunks, CHUNK_HEADS, rows), f32),
             pltpu.VMEM((cols, rows), f32),
-            pltpu.VMEM((chunks, 8, rows), f32),
+            pltpu.VMEM((chunks, CHUNK_HEADS, rows), f32),
             pltpu.VMEM((rows, cols), bf16),
             pltpu.VMEM(hyena_inputs.shape, bf16),
             pltpu.VMEM((2, RIM, cols), bf16),

time: 74.1 us -> 69.9 us (0.943)
  Pallas kernels: 71.7 us -> 67.4 us
    pallas_call x1, Pallas kernels: 71.7 us -> 67.4 us  [four_places(): pl.pallas_call(functools.partial(fused_kernel, ctx_size, heads_size), out...]
where the time goes in v4:
time: 69.9 us; the launch traced here: 69.8 us
  Pallas kernels  67.4 us (96%)
  local copies, waits for them, and re-layouts  2.3 us (3%)
    pallas_call x1, Pallas kernels, four_places(): pl.pallas_call(functools.partial(fused_kernel, ctx_size, heads_size), out...  67.4 us
    unnamed x1, local copies, waits for them, and re-layouts  2.3 us

profile of v4, /device:TPU:16, one launch (start us, length us, event | category | flops | bytes accessed | tf_op | source)
XLA Modules:
  0.0 69.8 jit_solution(12027832287939048630)
XLA Ops:
  0.0 67.4 %shard_map.64 = bf16[256,2048]{1,0:T(8,128)(2,1)} custom-call(bf16[256,2048]{1,0:T(8,128)(2,1)} %q_any.1, bf16[256,2048]{1,0:T(8,128)(2,1)} %k_any.1, bf16[256,2048]{1,0:T(8,128)(2,1)} %v_any.1, bf16[3,256,2048]{2,1,0:T(8,128)(2,1)} %hy_any.1, f32[7,2048]{1,0:T(8,128)} %filt_any.1, f32[1,2048]{1,0:T(1,128)} %bitcast.1), custom_call_target="tpu_custom_call" | custom-call | tf_op jit(solution)/shard_map/pallas_call | solution.py:468
  67.4 2.3 %copy.8 = bf16[256,2048]{1,0:T(8,128)(2,1)} copy(bf16[256,2048]{1,0:T(8,128)(2,1)} %shard_map.64) | data formatting | bytes 2097152

commit v5 on v4

--- a/solution.py
+++ b/solution.py
@@ -13,7 +13,7 @@
 MESH = pl.DeviceIdType.MESH
 LOG2E = 1.4426950408889634
 CHUNK_HEADS = 1
-DEPTH = 4
+DEPTH = 16
 LAG = 6
 RIM = 16
 K_UP, V_UP, K_SIDE, V_SIDE, Q_NEAR, Q_FAR, O_NEAR, O_FAR, S_NEAR, S_FAR, SINGLES, SQUARES = range(12)
@@ -189,9 +189,12 @@
         return (remote(q_own.at[:, at], q_far.at[1, :, at], Q_FAR, chunk, ctx - 4),) + near_copies(chunk)
 
     def begin(copies, depth):
-        for chunk in range(depth):
+        def step(chunk, carry):
             for copy in copies(chunk):
                 copy.start()
+            return carry
+
+        lax.fori_loop(0, min(depth, chunks), step, 0)
 
     def follow(copies, depth, chunk):
         for copy in copies(chunk):
@@ -203,8 +206,8 @@
                 copy.start()
 
     pl.when(place == 0)(lambda: begin(up_copies, DEPTH))
-    pl.when(place == 2)(lambda: begin(near_copies, 2 * DEPTH))
-    pl.when(place == 3)(lambda: begin(far_copies, 2 * DEPTH))
+    pl.when(place == 2)(lambda: begin(near_copies, DEPTH))
+    pl.when(place == 3)(lambda: begin(far_copies, DEPTH))
 
     def gate():
         @pl.when(ctx == 0)
@@ -374,7 +377,7 @@
     def _():
         @each_chunk
         def _(chunk):
-            follow(near_copies, 2 * DEPTH, chunk)
+            follow(near_copies, DEPTH, chunk)
             arrived(q_far.at[0, :, lanes(chunk)], Q_NEAR, chunk)
             for index in range(CHUNK_HEADS):
                 head = chunk * CHUNK_HEADS + index
@@ -393,7 +396,7 @@
     def _():
         @each_chunk
         def _(chunk):
-            follow(far_copies, 2 * DEPTH, chunk)
+            follow(far_copies, DEPTH, chunk)
             for index in range(CHUNK_HEADS):
                 head = chunk * CHUNK_HEADS + index
                 values = [turned(slot, head) for slot in (2, 3)]

time: 69.9 us -> 69.9 us (level)
  no operation moved by 1% of the time
where the time goes in v5:
time: 69.9 us; the launch traced here: 69.8 us
  Pallas kernels  67.4 us (96%)
  local copies, waits for them, and re-layouts  2.3 us (3%)
    pallas_call x1, Pallas kernels, four_places(): pl.pallas_call(functools.partial(fused_kernel, ctx_size, heads_size), out...  67.4 us
    unnamed x1, local copies, waits for them, and re-layouts  2.3 us

profile of v5, /device:TPU:16, one launch (start us, length us, event | category | flops | bytes accessed | tf_op | source)
XLA Modules:
  0.0 69.8 jit_solution(12103703726448455021)
XLA Ops:
  0.0 67.4 %shard_map.64 = bf16[256,2048]{1,0:T(8,128)(2,1)} custom-call(bf16[256,2048]{1,0:T(8,128)(2,1)} %q_any.1, bf16[256,2048]{1,0:T(8,128)(2,1)} %k_any.1, bf16[256,2048]{1,0:T(8,128)(2,1)} %v_any.1, bf16[3,256,2048]{2,1,0:T(8,128)(2,1)} %hy_any.1, f32[7,2048]{1,0:T(8,128)} %filt_any.1, f32[1,2048]{1,0:T(1,128)} %bitcast.1), custom_call_target="tpu_custom_call" | custom-call | tf_op jit(solution)/shard_map/pallas_call | solution.py:471
  67.5 2.3 %copy.8 = bf16[256,2048]{1,0:T(8,128)(2,1)} copy(bf16[256,2048]{1,0:T(8,128)(2,1)} %shard_map.64) | data formatting | bytes 2097152

commit v6 on v5

--- a/solution.py
+++ b/solution.py
@@ -209,30 +209,30 @@
     pl.when(place == 2)(lambda: begin(near_copies, DEPTH))
     pl.when(place == 3)(lambda: begin(far_copies, DEPTH))
 
-    def gate():
-        @pl.when(ctx == 0)
-        def _():
-            halo[...] = jnp.zeros_like(halo)
-
-        @pl.when(ctx > 0)
-        def _():
-            arrived(halo, SINGLES, 2)
-
-        for copy in local[:2]:
-            copy.wait()
-
+    def gate(count, rim):
         @each_chunk
         def _(chunk):
             at = lanes(chunk)
-            prod[:RIM] = halo[0, :, at].astype(jnp.float32) * halo[1, :, at].astype(jnp.float32)
-            prod[RIM:] = hy[1, :, at].astype(jnp.float32) * hy[2, :, at].astype(jnp.float32)
+            part = pl.ds(0, count)
+            if rim:
+                prod[:RIM] = halo[0, :, at].astype(jnp.float32) * halo[1, :, at].astype(jnp.float32)
+            else:
+                prod[:RIM] = jnp.zeros((RIM, wide), jnp.float32)
+            prod[RIM : RIM + count] = hy[1, part, at].astype(jnp.float32) * hy[2, part, at].astype(jnp.float32)
             taps = filt[:, at]
-            summed = taps[0:1] * prod[RIM : RIM + rows]
+            summed = taps[0:1] * prod[RIM : RIM + count]
             for tap in range(1, filt.shape[0]):
-                summed = summed + taps[tap : tap + 1] * prod[RIM - tap : RIM - tap + rows]
-            hyena[:, at] = hy[0, :, at].astype(jnp.float32) * summed
-
-    pl.when(place != 1)(gate)
+                summed = summed + taps[tap : tap + 1] * prod[RIM - tap : RIM - tap + count]
+            hyena[part, at] = hy[0, part, at].astype(jnp.float32) * summed
+
+    def redo_rim():
+        arrived(halo, SINGLES, 2)
+        gate(RIM, True)
+
+    for copy in local[:2]:
+        copy.wait()
+    gate(rows, False)
+    pl.when(place >= 2)(redo_rim)
 
     local[5].wait()
     arrived(k_all.at[2], SINGLES, 0)
@@ -334,18 +334,24 @@
                 finish(head, attend_some(head, own_query(head), (2, 3), values, True)[0])
 
         pl.when(core == 1)(send_tail)
+        pl.when(core == 1)(redo_rim)
 
     @pl.when(place == 1)
     def _():
-        @each_chunk
-        def _(chunk):
+        def forward(chunk):
             at = lanes(chunk)
             arrived(k_all.at[core, :, at], K_UP, chunk)
             remote(k_all.at[core, :, at], k_all.at[core, :, at], K_SIDE, chunk, side).start()
             arrived(v_all.at[core, :, at], V_UP, chunk)
             remote(v_all.at[core, :, at], v_all.at[core, :, at], V_SIDE, chunk, side).start()
+
+        forward(0)
+
+        @each_chunk
+        def _(chunk):
+            at = lanes(chunk)
+            arrived(q_far.at[1, :, at], Q_FAR, chunk)
             arrived(q_far.at[0, :, at], Q_NEAR, chunk)
-            arrived(q_far.at[1, :, at], Q_FAR, chunk)
             arrived(k_all.at[1 - core, :, at], K_SIDE, chunk)
             arrived(v_all.at[1 - core, :, at], V_SIDE, chunk)
             slots = (0, 1, 2, 3)
@@ -370,8 +376,10 @@
                 partial_out(far, chunk, index, heads[index], result)
                 if index == CHUNK_HEADS - 1:
                     send_out(far, chunk, far, ctx + 2 + 2 * far)
-
-        gate()
+                    if far == 0:
+                        pl.when(chunk + 1 < chunks)(lambda: forward(chunk + 1))
+
+        redo_rim()
 
     @pl.when(place == 2)
     def _():
@@ -497,7 +505,7 @@
             pltpu.SemaphoreType.DMA((6,)),
         ],
         compiler_params=pltpu.CompilerParams(
-            collective_id=0, has_side_effects=True, vmem_limit_bytes=63 * 1024 * 1024
+            collective_id=0, has_side_effects=True, vmem_limit_bytes=52 * 1024 * 1024
         ),
     )(queries, keys, values, hyena_inputs, hyena_filter, norm_gain[None, :])
 

time: 69.9 us -> 69 us (0.987)
  Pallas kernels: 67.4 us -> 66.3 us
    pallas_call x1, Pallas kernels: 67.4 us -> 66.3 us  [four_places(): pl.pallas_call(functools.partial(fused_kernel, ctx_size, heads_size), out...]
    unnamed x1 -> x5, local copies, waits for them, and re-layouts: 2.3 us -> 2.51 us
where the time goes in v6:
time: 69 us; the launch traced here: 68.9 us
  Pallas kernels  66.3 us (96%)
  local copies, waits for them, and re-layouts  2.51 us (4%)
    pallas_call x1, Pallas kernels, four_places(): pl.pallas_call(functools.partial(fused_kernel, ctx_size, heads_size), out...  66.3 us
    unnamed x5, local copies, waits for them, and re-layouts  2.51 us

profile of v6, /device:TPU:16, one launch (start us, length us, event | category | flops | bytes accessed | tf_op | source)
XLA Modules:
  0.0 68.9 jit_solution(12422182544780644059)
XLA Ops:
  0.0 0.0 copy-start
  0.0 0.8 %copy-done = f32[7,2048]{1,0:T(8,128)S(1)} copy-done((f32[7,2048]{1,0:T(8,128)S(1)}, f32[7,2048]{1,0:T(8,128)}, u32[]{:S(2)}) %copy-start) | copy-done | bytes 57368
  0.8 0.0 copy-start.1
  0.8 0.7 %copy-done.1 = f32[2048]{0:T(1024)S(1)} copy-done((f32[2048]{0:T(1024)S(1)}, f32[2048]{0:T(1024)}, u32[]{:S(2)}) %copy-start.1) | copy-done | bytes 8216
  1.5 66.3 %shard_map.64 = bf16[256,2048]{1,0:T(8,128)(2,1)S(1)} custom-call(bf16[256,2048]{1,0:T(8,128)(2,1)} %q_any.1, bf16[256,2048]{1,0:T(8,128)(2,1)} %k_any.1, bf16[256,2048]{1,0:T(8,128)(2,1)} %v_any.1, bf16[3,256,2048]{2,1,0:T(8,128)(2,1)} %hy_any.1, f32[7,2048]{1,0:T(8,128)S(1)} %copy-done, f32[1,2048]{1,0:T(1,128)S(1)} %bitcast.1), custom_call_target="tpu_custom_call" | custom-call | tf_op jit(solution)/shard_map/pallas_call | solution.py:479
  67.9 1.0 %copy.8 = bf16[256,2048]{1,0:T(8,128)(2,1)} copy(bf16[256,2048]{1,0:T(8,128)(2,1)S(1)} %shard_map.64) | data formatting | bytes 2097152
Async XLA Ops:
  0.0 0.8 %copy-start = (f32[7,2048]{1,0:T(8,128)S(1)}, f32[7,2048]{1,0:T(8,128)}, u32[]{:S(2)}) copy-start(f32[7,2048]{1,0:T(8,128)} %filt_any.1) | copy-start | bytes 172036
  0.8 0.7 %copy-start.1 = (f32[2048]{0:T(1024)S(1)}, f32[2048]{0:T(1024)}, u32[]{:S(2)}) copy-start(f32[2048]{0:T(1024)} %param.11) | copy-start | bytes 24580

commit v7 on v6

--- a/solution.py
+++ b/solution.py
@@ -13,10 +13,10 @@
 MESH = pl.DeviceIdType.MESH
 LOG2E = 1.4426950408889634
 CHUNK_HEADS = 1
-DEPTH = 16
 LAG = 6
 RIM = 16
 K_UP, V_UP, K_SIDE, V_SIDE, Q_NEAR, Q_FAR, O_NEAR, O_FAR, S_NEAR, S_FAR, SINGLES, SQUARES = range(12)
+K_SIB, V_SIB = 12, 13
 
 
 def from_behind(array, axis, by):
@@ -169,10 +169,6 @@
     def send_tail():
         remote(tail, halo, SINGLES, 2, ctx + 1).start()
 
-    pl.when((ctx < ctx_size - 1) & (ctx != 1))(send_tail)
-    remote(k_any, k_all.at[2 + core], SINGLES, 0, side).start()
-    remote(v_any, v_all.at[2 + core], SINGLES, 1, side).start()
-
     def up_copies(chunk):
         at = lanes(chunk)
         return (
@@ -188,26 +184,28 @@
         at = lanes(chunk)
         return (remote(q_own.at[:, at], q_far.at[1, :, at], Q_FAR, chunk, ctx - 4),) + near_copies(chunk)
 
-    def begin(copies, depth):
-        def step(chunk, carry):
+    def sibling_copies(chunk):
+        at = lanes(chunk)
+        return (
+            remote(k_all.at[2 + core, :, at], k_all.at[2 + core, :, at], K_SIB, chunk, side),
+            remote(v_all.at[2 + core, :, at], v_all.at[2 + core, :, at], V_SIB, chunk, side),
+        )
+
+    def sibling_arrived(chunk):
+        arrived(k_all.at[3 - core, :, lanes(chunk)], K_SIB, chunk)
+        arrived(v_all.at[3 - core, :, lanes(chunk)], V_SIB, chunk)
+
+    @each_chunk
+    def _(chunk):
+        def begin(copies):
             for copy in copies(chunk):
                 copy.start()
-            return carry
-
-        lax.fori_loop(0, min(depth, chunks), step, 0)
-
-    def follow(copies, depth, chunk):
-        for copy in copies(chunk):
-            copy.wait_send()
-
-        @pl.when(chunk + depth < chunks)
-        def _():
-            for copy in copies(chunk + depth):
-                copy.start()
-
-    pl.when(place == 0)(lambda: begin(up_copies, DEPTH))
-    pl.when(place == 2)(lambda: begin(near_copies, DEPTH))
-    pl.when(place == 3)(lambda: begin(far_copies, DEPTH))
+
+        pl.when(place == 0)(lambda: begin(up_copies))
+        pl.when(place == 2)(lambda: begin(near_copies))
+        pl.when(place == 3)(lambda: begin(far_copies))
+        begin(sibling_copies)
+        pl.when((ctx < ctx_size - 1) & (ctx != 1) & (chunk == 1))(send_tail)
 
     def gate(count, rim):
         @each_chunk
@@ -232,11 +230,8 @@
     for copy in local[:2]:
         copy.wait()
     gate(rows, False)
-    pl.when(place >= 2)(redo_rim)
 
     local[5].wait()
-    arrived(k_all.at[2], SINGLES, 0)
-    arrived(v_all.at[2], SINGLES, 1)
     squares[mine] = jnp.zeros_like(squares[mine])
 
     key_place = lax.broadcasted_iota(jnp.int32, (rows, rows), 0)
@@ -327,7 +322,7 @@
     def _():
         @each_chunk
         def _(chunk):
-            follow(up_copies, DEPTH, chunk)
+            sibling_arrived(chunk)
             for index in range(CHUNK_HEADS):
                 head = chunk * CHUNK_HEADS + index
                 values = [turned(slot, head) for slot in (2, 3)]
@@ -350,6 +345,7 @@
         @each_chunk
         def _(chunk):
             at = lanes(chunk)
+            sibling_arrived(chunk)
             arrived(q_far.at[1, :, at], Q_FAR, chunk)
             arrived(q_far.at[0, :, at], Q_NEAR, chunk)
             arrived(k_all.at[1 - core, :, at], K_SIDE, chunk)
@@ -385,7 +381,7 @@
     def _():
         @each_chunk
         def _(chunk):
-            follow(near_copies, DEPTH, chunk)
+            sibling_arrived(chunk)
             arrived(q_far.at[0, :, lanes(chunk)], Q_NEAR, chunk)
             for index in range(CHUNK_HEADS):
                 head = chunk * CHUNK_HEADS + index
@@ -398,13 +394,14 @@
             send_out(0, chunk, 0, ctx + 2)
             merge_behind((0,), chunk)
 
+        redo_rim()
         merge_rest((0,))
 
     @pl.when(place == 3)
     def _():
         @each_chunk
         def _(chunk):
-            follow(far_copies, DEPTH, chunk)
+            sibling_arrived(chunk)
             for index in range(CHUNK_HEADS):
                 head = chunk * CHUNK_HEADS + index
                 values = [turned(slot, head) for slot in (2, 3)]
@@ -413,6 +410,7 @@
                 s_home[chunk, index : index + 1, :] = log_total
             merge_behind((0, 1), chunk)
 
+        redo_rim()
         merge_rest((0, 1))
 
     def square_copy(step, slot):
@@ -446,9 +444,6 @@
     def _():
         sent(tail, SINGLES, 2)
 
-    sent(k_any, SINGLES, 0)
-    sent(v_any, SINGLES, 1)
-
     def sent_lanes(kinds):
         @each_chunk
         def _(chunk):
@@ -462,6 +457,10 @@
                 sent(o_put.at[slot, chunk_rows(chunk)], O_NEAR + slot, chunk)
                 sent(s_put.at[slot, chunk], S_NEAR + slot, chunk)
 
+    sent_lanes((K_SIB, V_SIB))
+    pl.when(place == 0)(lambda: sent_lanes((K_UP, V_UP)))
+    pl.when(place == 2)(lambda: sent_lanes((Q_NEAR,)))
+    pl.when(place == 3)(lambda: sent_lanes((Q_NEAR, Q_FAR)))
     pl.when(place == 2)(lambda: sent_out((0,)))
 
     @pl.when(place == 1)
@@ -500,8 +499,8 @@
             pltpu.VMEM((heads_size, 8, rows), f32),
             pltpu.VMEM(hyena_filter.shape, f32),
             pltpu.VMEM((1, cols), f32),
-            pltpu.SemaphoreType.DMA((12, count)),
-            pltpu.SemaphoreType.DMA((12, count)),
+            pltpu.SemaphoreType.DMA((14, count)),
+            pltpu.SemaphoreType.DMA((14, count)),
             pltpu.SemaphoreType.DMA((6,)),
         ],
         compiler_params=pltpu.CompilerParams(

time: 69 us -> 69.9 us (1.013)
  Pallas kernels: 66.3 us -> 67.1 us
    pallas_call x1, Pallas kernels: 66.3 us -> 67.1 us  [four_places(): pl.pallas_call(functools.partial(fused_kernel, ctx_size, heads_size), out...]
where the time goes in v7:
time: 69.9 us; the launch traced here: 69.7 us
  Pallas kernels  67.1 us (96%)
  local copies, waits for them, and re-layouts  2.51 us (4%)
    pallas_call x1, Pallas kernels, four_places(): pl.pallas_call(functools.partial(fused_kernel, ctx_size, heads_size), out...  67.1 us
    unnamed x5, local copies, waits for them, and re-layouts  2.51 us

profile of v7, /device:TPU:16, one launch (start us, length us, event | category | flops | bytes accessed | tf_op | source)
XLA Modules:
  0.0 69.7 jit_solution(2977129052217574410)
XLA Ops:
  0.0 0.0 copy-start
  0.0 0.8 %copy-done = f32[7,2048]{1,0:T(8,128)S(1)} copy-done((f32[7,2048]{1,0:T(8,128)S(1)}, f32[7,2048]{1,0:T(8,128)}, u32[]{:S(2)}) %copy-start) | copy-done | bytes 57368
  0.8 0.0 copy-start.1
  0.8 0.7 copy-done.1
  1.5 67.1 %shard_map.64 = bf16[256,2048]{1,0:T(8,128)(2,1)S(1)} custom-call(bf16[256,2048]{1,0:T(8,128)(2,1)} %q_any.1, bf16[256,2048]{1,0:T(8,128)(2,1)} %k_any.1, bf16[256,2048]{1,0:T(8,128)(2,1)} %v_any.1, bf16[3,256,2048]{2,1,0:T(8,128)(2,1)} %hy_any.1, f32[7,2048]{1,0:T(8,128)S(1)} %copy-done, f32[1,2048]{1,0:T(1,128)S(1)} %bitcast.1), custom_call_target="tpu_custom_call" | custom-call | tf_op jit(solution)/shard_map/pallas_call | solution.py:478
  68.7 1.0 %copy.8 = bf16[256,2048]{1,0:T(8,128)(2,1)} copy(bf16[256,2048]{1,0:T(8,128)(2,1)S(1)} %shard_map.64) | data formatting | bytes 2097152
Async XLA Ops:
  0.0 0.8 %copy-start = (f32[7,2048]{1,0:T(8,128)S(1)}, f32[7,2048]{1,0:T(8,128)}, u32[]{:S(2)}) copy-start(f32[7,2048]{1,0:T(8,128)} %filt_any.1) | copy-start | bytes 172036
  0.8 0.7 %copy-start.1 = (f32[2048]{0:T(1024)S(1)}, f32[2048]{0:T(1024)}, u32[]{:S(2)}) copy-start(f32[2048]{0:T(1024)} %param.11) | copy-start | bytes 24580

commit v8 on v7

--- a/solution.py
+++ b/solution.py
@@ -14,6 +14,7 @@
 LOG2E = 1.4426950408889634
 CHUNK_HEADS = 1
 LAG = 6
+OWN_LATE = 4
 RIM = 16
 K_UP, V_UP, K_SIDE, V_SIDE, Q_NEAR, Q_FAR, O_NEAR, O_FAR, S_NEAR, S_FAR, SINGLES, SQUARES = range(12)
 K_SIB, V_SIB = 12, 13
@@ -340,6 +341,14 @@
             arrived(v_all.at[core, :, at], V_UP, chunk)
             remote(v_all.at[core, :, at], v_all.at[core, :, at], V_SIDE, chunk, side).start()
 
+        slots = (0, 1, 2, 3)
+
+        def own(chunk):
+            for index in range(CHUNK_HEADS):
+                head = chunk * CHUNK_HEADS + index
+                values = [turned(slot, head) for slot in slots]
+                finish(head, attend_some(head, own_query(head), slots, values, True)[0])
+
         forward(0)
 
         @each_chunk
@@ -350,31 +359,29 @@
             arrived(q_far.at[0, :, at], Q_NEAR, chunk)
             arrived(k_all.at[1 - core, :, at], K_SIDE, chunk)
             arrived(v_all.at[1 - core, :, at], V_SIDE, chunk)
-            slots = (0, 1, 2, 3)
             heads = [chunk * CHUNK_HEADS + index for index in range(CHUNK_HEADS)]
             values = [[turned(slot, head) for slot in slots] for head in heads]
-            works = [(far, index) for far in (1, 0, None) for index in range(CHUNK_HEADS)]
+            works = [(far, index) for far in (1, 0) for index in range(CHUNK_HEADS)]
 
             def begin_work(far, index):
-                head = heads[index]
-                query = own_query(head) if far is None else q_far[far, :, head_lanes(head)]
-                return masked_scores(head, query, slots, far is None)
+                return masked_scores(heads[index], q_far[far, :, head_lanes(heads[index])], slots, False)
 
             ready = begin_work(*works[0])
             for number, (far, index) in enumerate(works):
                 current = ready
                 if number + 1 < len(works):
                     ready = begin_work(*works[number + 1])
-                result = weigh(*current, values[index])
-                if far is None:
-                    finish(heads[index], result[0])
-                    continue
-                partial_out(far, chunk, index, heads[index], result)
+                partial_out(far, chunk, index, heads[index], weigh(*current, values[index]))
                 if index == CHUNK_HEADS - 1:
                     send_out(far, chunk, far, ctx + 2 + 2 * far)
-                    if far == 0:
-                        pl.when(chunk + 1 < chunks)(lambda: forward(chunk + 1))
-
+            pl.when(chunk + 1 < chunks)(lambda: forward(chunk + 1))
+            pl.when(chunk < chunks - OWN_LATE)(lambda: own(chunk))
+
+        def late(chunk, carry):
+            own(chunk)
+            return carry
+
+        lax.fori_loop(max(chunks - OWN_LATE, 0), chunks, late, 0)
         redo_rim()
 
     @pl.when(place == 2)

time: 69.9 us -> 69.9 us (level)
  no operation moved by 1% of the time
where the time goes in v8:
time: 69.9 us; the launch traced here: 69.7 us
  Pallas kernels  67.2 us (96%)
  local copies, waits for them, and re-layouts  2.51 us (4%)
    pallas_call x1, Pallas kernels, four_places(): pl.pallas_call(functools.partial(fused_kernel, ctx_size, heads_size), out...  67.2 us
    unnamed x5, local copies, waits for them, and re-layouts  2.51 us

profile of v8, /device:TPU:16, one launch (start us, length us, event | category | flops | bytes accessed | tf_op | source)
XLA Modules:
  0.0 69.7 jit_solution(4126597880651469874)
XLA Ops:
  0.0 0.0 copy-start
  0.0 0.8 %copy-done = f32[7,2048]{1,0:T(8,128)S(1)} copy-done((f32[7,2048]{1,0:T(8,128)S(1)}, f32[7,2048]{1,0:T(8,128)}, u32[]{:S(2)}) %copy-start) | copy-done | bytes 57368
  0.8 0.0 copy-start.1
  0.8 0.7 copy-done.1
  1.5 67.2 %shard_map.64 = bf16[256,2048]{1,0:T(8,128)(2,1)S(1)} custom-call(bf16[256,2048]{1,0:T(8,128)(2,1)} %q_any.1, bf16[256,2048]{1,0:T(8,128)(2,1)} %k_any.1, bf16[256,2048]{1,0:T(8,128)(2,1)} %v_any.1, bf16[3,256,2048]{2,1,0:T(8,128)(2,1)} %hy_any.1, f32[7,2048]{1,0:T(8,128)S(1)} %copy-done, f32[1,2048]{1,0:T(1,128)S(1)} %bitcast.1), custom_call_target="tpu_custom_call" | custom-call | tf_op jit(solution)/shard_map/pallas_call | solution.py:485
  68.8 1.0 %copy.8 = bf16[256,2048]{1,0:T(8,128)(2,1)} copy(bf16[256,2048]{1,0:T(8,128)(2,1)S(1)} %shard_map.64) | data formatting | bytes 2097152
Async XLA Ops:
  0.0 0.8 %copy-start = (f32[7,2048]{1,0:T(8,128)S(1)}, f32[7,2048]{1,0:T(8,128)}, u32[]{:S(2)}) copy-start(f32[7,2048]{1,0:T(8,128)} %filt_any.1) | copy-start | bytes 172036
  0.8 0.7 copy-start.1

commit v9 on v6

--- a/solution.py
+++ b/solution.py
@@ -14,7 +14,8 @@
 LOG2E = 1.4426950408889634
 CHUNK_HEADS = 1
 DEPTH = 16
-LAG = 6
+LAG = 8
+GROUP = 4
 RIM = 16
 K_UP, V_UP, K_SIDE, V_SIDE, Q_NEAR, Q_FAR, O_NEAR, O_FAR, S_NEAR, S_FAR, SINGLES, SQUARES = range(12)
 
@@ -292,12 +293,22 @@
     def send_out(slot, chunk, to_slot, target):
         at = chunk_rows(chunk)
         remote(o_put.at[slot, at], o_got.at[to_slot, at], O_NEAR + to_slot, chunk, target).start()
-        remote(s_put.at[slot, chunk], s_got.at[to_slot, chunk], S_NEAR + to_slot, chunk, target).start()
+
+        @pl.when(lax.rem(chunk, GROUP) == GROUP - 1)
+        def _():
+            logs = pl.ds(chunk - (GROUP - 1), GROUP)
+            remote(
+                s_put.at[slot, logs], s_got.at[to_slot, logs], S_NEAR + to_slot, chunk // GROUP, target
+            ).start()
 
     def merge(slots, chunk):
         for slot in slots:
             arrived(o_got.at[slot, chunk_rows(chunk)], O_NEAR + slot, chunk)
-            arrived(s_got.at[slot, chunk], S_NEAR + slot, chunk)
+
+            @pl.when(lax.rem(chunk, GROUP) == 0)
+            def _():
+                arrived(s_got.at[slot, pl.ds(chunk, GROUP)], S_NEAR + slot, chunk // GROUP)
+
         for index in range(CHUNK_HEADS):
             head = chunk * CHUNK_HEADS + index
             logs = [s_home[chunk, index : index + 1, :]]
@@ -460,7 +471,11 @@
         def _(chunk):
             for slot in slots:
                 sent(o_put.at[slot, chunk_rows(chunk)], O_NEAR + slot, chunk)
-                sent(s_put.at[slot, chunk], S_NEAR + slot, chunk)
+
+                @pl.when(lax.rem(chunk, GROUP) == 0)
+                def _():
+                    sent(s_put.at[slot, pl.ds(chunk, GROUP)], S_NEAR + slot, chunk // GROUP)
+
 
     pl.when(place == 2)(lambda: sent_out((0,)))
 

time: 69 us -> 69.6 us (level)
  no operation moved by 1% of the time
where the time goes in v9:
time: 69.6 us; the launch traced here: 69.4 us
  Pallas kernels  66.9 us (96%)
  local copies, waits for them, and re-layouts  2.51 us (4%)
    pallas_call x1, Pallas kernels, four_places(): pl.pallas_call(functools.partial(fused_kernel, ctx_size, heads_size), out...  66.9 us
    unnamed x5, local copies, waits for them, and re-layouts  2.51 us

profile of v9, /device:TPU:16, one launch (start us, length us, event | category | flops | bytes accessed | tf_op | source)
XLA Modules:
  0.0 69.4 jit_solution(13381060199620434462)
XLA Ops:
  0.0 0.0 copy-start
  0.0 0.8 %copy-done = f32[7,2048]{1,0:T(8,128)S(1)} copy-done((f32[7,2048]{1,0:T(8,128)S(1)}, f32[7,2048]{1,0:T(8,128)}, u32[]{:S(2)}) %copy-start) | copy-done | bytes 57368
  0.8 0.0 copy-start.1
  0.8 0.7 %copy-done.1 = f32[2048]{0:T(1024)S(1)} copy-done((f32[2048]{0:T(1024)S(1)}, f32[2048]{0:T(1024)}, u32[]{:S(2)}) %copy-start.1) | copy-done | bytes 8216
  1.5 66.9 %shard_map.64 = bf16[256,2048]{1,0:T(8,128)(2,1)S(1)} custom-call(bf16[256,2048]{1,0:T(8,128)(2,1)} %q_any.1, bf16[256,2048]{1,0:T(8,128)(2,1)} %k_any.1, bf16[256,2048]{1,0:T(8,128)(2,1)} %v_any.1, bf16[3,256,2048]{2,1,0:T(8,128)(2,1)} %hy_any.1, f32[7,2048]{1,0:T(8,128)S(1)} %copy-done, f32[1,2048]{1,0:T(1,128)S(1)} %bitcast.1), custom_call_target="tpu_custom_call" | custom-call | tf_op jit(solution)/shard_map/pallas_call | solution.py:494
  68.5 1.0 %copy.8 = bf16[256,2048]{1,0:T(8,128)(2,1)} copy(bf16[256,2048]{1,0:T(8,128)(2,1)S(1)} %shard_map.64) | data formatting | bytes 2097152
Async XLA Ops:
  0.0 0.8 %copy-start = (f32[7,2048]{1,0:T(8,128)S(1)}, f32[7,2048]{1,0:T(8,128)}, u32[]{:S(2)}) copy-start(f32[7,2048]{1,0:T(8,128)} %filt_any.1) | copy-start | bytes 172036
  0.8 0.7 %copy-start.1 = (f32[2048]{0:T(1024)S(1)}, f32[2048]{0:T(1024)}, u32[]{:S(2)}) copy-start(f32[2048]{0:T(1024)} %param.11) | copy-start | bytes 24580
